TPU v7x, 256 devices: a whole 4x4x8 slice. The times are simulated.
256 devices in a mesh: seq: 16 (over z_hi, y, core), pipe: 16 (over x, z_lo).
Axes of the slice: x: 4, y: 4, z: 8 (z_hi: 2, z_lo: 4; z = z_hi * 4 + z_lo), core: 2. Of those that a mesh axis runs over, the one named last changes fastest.
Arguments:
- acts: bfloat16 [16, 2048, 2048], P('pipe', 'seq'), may hold values from -6 to 6
- norm_gain: float32 [16, 2048], P('pipe'), may hold values from 0.25 to 1.75
- query_weight: bfloat16 [16, 2048, 2048], P('pipe', None, 'seq'), may hold values from -64 to 64
- kv_weight: bfloat16 [16, 2048, 1024], P('pipe', None, 'seq'), may hold values from -64 to 64
- out_weight: bfloat16 [16, 2048, 2048], P('pipe', 'seq'), may hold values from -0.125 to 0.125
- first_values: bfloat16 [16, 2048, 512], P('pipe', 'seq'), may hold values from -6 to 6
- mix_weight: float32 [16, 8], P('pipe'), may hold values from 0.2 to 0.8
Outputs:
- passed: bfloat16 [16, 2048, 2048], P('pipe', 'seq')
- fresh_values: bfloat16 [16, 2048, 512], P('pipe', 'seq')
All inputs are finite; a program needn't handle non-finite values.
Results may differ from a plain program's by a relative error of at most 0.011.
Values may be sent and summed in bfloat16 or wider, within the bound.
No kernel may reach another device: no remote copies, remote signals or barrier semaphores. Data moves between devices by JAX's collectives and lax.ppermute only.
A program may use at most 128 MiB of HBM per device.

v0:
```python
import jax
import jax.numpy as jnp
from jax import lax
from jax.sharding import PartitionSpec as P

rope_base = 500000.0


def from_root(x, axis, root):
    mine = lax.axis_index(axis) == root
    return lax.psum(jnp.where(mine, x, jnp.zeros_like(x)), axis)


def passed_along(x, axis, by):
    peers = lax.axis_size(axis)
    return lax.ppermute(x, axis, [(i, (i + by) % peers) for i in range(peers)])


def block_rows():
    return 512


def normalize(inputs, gain):
    wide = inputs.astype(jnp.float32)
    scale = lax.rsqrt(jnp.mean(wide * wide, axis=-1, keepdims=True) + 1e-05)
    return (wide * scale * gain).astype(jnp.bfloat16)


def rotate(heads_in, positions):
    width = heads_in.shape[-1]
    half = width // 2
    freq = rope_base ** (-2.0 * jnp.arange(half, dtype=jnp.float32) / width)
    angle = positions.astype(jnp.float32)[:, None, None] * freq
    cosine = jnp.cos(angle)
    sine = jnp.sin(angle)
    lower = heads_in[..., :half]
    upper = heads_in[..., half:]
    return jnp.concatenate([lower * cosine - upper * sine, upper * cosine + lower * sine], axis=-1)


def attend(own_queries, own_keys, own_values):
    all_rows, local_heads, head_dim = own_queries.shape
    kv_local = own_keys.shape[1]
    group = local_heads // kv_local
    grouped = own_queries.reshape(all_rows, kv_local, group, head_dim)
    block = block_rows()
    scale = head_dim ** (-0.5)
    outputs = []
    for begin in range(0, all_rows, block):
        finish = begin + block
        scores = (
            jnp.einsum(
                "qkgd,skd->kgqs",
                grouped[begin:finish],
                own_keys[:finish],
                preferred_element_type=jnp.float32,
            )
            * scale
        )
        row_ids = begin + jnp.arange(block, dtype=jnp.int32)[:, None]
        col_ids = jnp.arange(finish, dtype=jnp.int32)[None, :]
        scores = jnp.where(col_ids <= row_ids, scores, -1e30)
        top_score = jnp.max(scores, axis=-1, keepdims=True)
        weights = jnp.exp(scores - top_score)
        probs = (weights / jnp.sum(weights, axis=-1, keepdims=True)).astype(jnp.bfloat16)
        result = jnp.einsum(
            "kgqs,skd->qkgd", probs, own_values[:finish], preferred_element_type=jnp.float32
        ).astype(jnp.bfloat16)
        outputs.append(result.reshape(block, local_heads, head_dim))
    return jnp.concatenate(outputs, axis=0)


def per_device(acts, norm_gain, query_weight, kv_weight, out_weight, first_values, mix_weight):
    inputs = acts[0]
    tok_rows = inputs.shape[0]
    seq_parts = lax.axis_size("seq")
    seq_index = lax.axis_index("seq")
    section_index = lax.axis_index("pipe")
    kv_heads = mix_weight.shape[1]
    kv_width = first_values.shape[2]
    head_dim = kv_width // kv_heads
    head_count = out_weight.shape[1] * seq_parts // head_dim
    normed = normalize(inputs, norm_gain[0])
    positions = seq_index * tok_rows + jnp.arange(tok_rows, dtype=jnp.int32)

    def project(piece):
        return jnp.dot(normed, piece, preferred_element_type=jnp.float32)

    keyval = project(lax.all_gather(kv_weight[0], "seq", axis=1, tiled=True))
    keys_rot = rotate(keyval[:, :kv_width].reshape(tok_rows, kv_heads, head_dim), positions).astype(
        jnp.bfloat16
    )
    values = keyval[:, kv_width:].astype(jnp.bfloat16)
    fresh_vals = from_root(values, "pipe", 0)
    first_vals = jnp.where(section_index == 0, values, first_values[0])
    lam_cols = jnp.repeat(mix_weight[0], head_dim)
    mixed_vals = (
        lam_cols * values.astype(jnp.float32) + (1.0 - lam_cols) * first_vals.astype(jnp.float32)
    ).astype(jnp.bfloat16)
    mixed_vals = mixed_vals.reshape(tok_rows, kv_heads, head_dim)
    copies = max(1, seq_parts // kv_heads)
    keys_wide = jnp.repeat(keys_rot, copies, axis=1)
    values_wide = jnp.repeat(mixed_vals, copies, axis=1)
    query_proj = project(lax.all_gather(query_weight[0], "seq", axis=1, tiled=True))
    queries = rotate(query_proj.reshape(tok_rows, head_count, head_dim), positions).astype(
        jnp.bfloat16
    )
    own_queries, own_keys, own_values = (
        lax.all_to_all(queries, "seq", split_axis=1, concat_axis=0, tiled=True),
        lax.all_to_all(keys_wide, "seq", split_axis=1, concat_axis=0, tiled=True),
        lax.all_to_all(values_wide, "seq", split_axis=1, concat_axis=0, tiled=True),
    )
    attended = attend(own_queries, own_keys, own_values)
    regrouped = lax.all_to_all(attended, "seq", split_axis=0, concat_axis=1, tiled=True).reshape(
        tok_rows, head_count * head_dim
    )
    projected = jnp.dot(
        regrouped,
        lax.all_gather(out_weight[0], "seq", axis=0, tiled=True),
        preferred_element_type=jnp.float32,
    )
    layer_out = (inputs.astype(jnp.float32) + projected).astype(jnp.bfloat16)
    passed = passed_along(layer_out, "pipe", 1)
    return (passed[None], fresh_vals[None])


def solution(mesh):
    placed = (
        P("pipe", "seq", None),
        P("pipe", None),
        P("pipe", None, "seq"),
        P("pipe", None, "seq"),
        P("pipe", "seq", None),
        P("pipe", "seq", None),
        P("pipe", None),
    )
    return jax.shard_map(
        per_device,
        mesh=mesh,
        in_specs=placed,
        out_specs=(P("pipe", "seq", None), P("pipe", "seq", None)),
        check_vma=False,
    )
```

profile of v0, /device:TPU:136, one launch (start us, length us, event | category | flops | bytes accessed | tf_op | source)
XLA Modules:
  0.0 501.6 jit_solution(11465642980817413339)
XLA Ops:
  10.2 1.2 fusion.44
  11.6 66.5 %all-gather.7.cloned.1.call-done = bf16[1,2048,1024]{1,2,0:T(8,128)(2,1)} async-done(((bf16[1,2048,64]{1,2,0:T(8,128)(2,1)}), bf16[1,2048,1024]{1,2,0:T(8,128)(2,1)}) %all-gather.7.cloned.1.call-update) | async-done | bytes 4194320 | tf_op jit(solution)/shard_map/all_gather | solution.py:89
  78.1 3.9 fusion.8
  83.9 15.3 %all-to-all-start.1 = ((bf16[128,16,64]{0,2,1:T(8,128)(2,1)}), bf16[128,16,64]{0,2,1:T(8,128)(2,1)S(1)}, u32[]{:S(2)}, u32[]{:S(2)}) async-start(bf16[128,16,64]{0,2,1:T(8,128)(2,1)} %bitcast.10), calls=%async_computation.1 | async-start | bytes 524288 | tf_op jit(solution)/shard_map/all_to_all | solution.py:110
  100.5 89.7 %all-gather.9.cloned.1.call-done = bf16[1,2048,2048]{2,1,0:T(8,128)(2,1)} async-done(((bf16[1,2048,128]{2,1,0:T(8,128)(2,1)}), bf16[1,2048,2048]{2,1,0:T(8,128)(2,1)}) %all-gather.9.cloned.1.call-update) | async-done | bytes 8388624 | tf_op jit(solution)/shard_map/all_gather | solution.py:104
  190.2 12.4 %copy.60 = bf16[2048,2048]{1,0:T(8,128)(2,1)} copy(bf16[2048,2048]{0,1:T(8,128)(2,1)} %bitcast.226) | data formatting | bytes 16777216 | tf_op jit(solution)/shard_map/dot_general | solution.py:87
  203.4 20.2 %all-to-all-start = ((bf16[128,16,64]{0,2,1:T(8,128)(2,1)}), bf16[128,16,64]{0,2,1:T(8,128)(2,1)S(1)}, u32[]{:S(2)}, u32[]{:S(2)}) async-start(bf16[128,16,64]{0,2,1:T(8,128)(2,1)} %bitcast.6), calls=%async_computation | async-start | bytes 524288 | tf_op jit(solution)/shard_map/all_to_all | solution.py:111
  223.6 5.9 %fusion.51 = f32[128,32,64]{0,2,1:T(8,128)S(1)} fusion(bf16[32,64,2048]{2,1,0:T(8,128)(2,1)} %bitcast.225, bf16[1,128,2048]{2,1,0:T(8,128)(2,1)S(1)} %copy-done, f32[2048]{0:T(1024)S(1)} %bitcast.241, f32[128]{0:T(128)S(1)} %add_rsqrt_fusion), kind=kOutput, calls=%fused_computation.54 | convolution fusion | flops 1074790400 | bytes 9970176 | tf_op jit(solution)/shard_map/dot_general | solution.py:87
  230.5 2.3 all-to-all-done
  232.8 15.3 %all-to-all-start.2 = ((bf16[128,32,64]{0,2,1:T(8,128)(2,1)}), bf16[128,32,64]{0,2,1:T(8,128)(2,1)}, u32[]{:S(2)}, u32[]{:S(2)}) async-start(bf16[128,32,64]{0,2,1:T(8,128)(2,1)} %pad_maximum_fusion), calls=%async_computation.2 | async-start | bytes 1048576 | tf_op jit(solution)/shard_map/all_to_all | solution.py:109
  256.5 1.0 copy.64
  258.4 1.1 copy.68
  260.3 1.1 copy.67
  262.2 1.1 reshape.316
  263.2 1.1 reshape.317
  264.3 1.2 slice_bitcast_fusion.3
  265.5 1.6 fusion.76
  267.4 1.0 fusion.11
  268.9 1.0 fusion.10
  269.9 1.3 fusion.5
  271.2 1.8 fusion.3
  273.1 1.5 fusion.4
  274.6 2.2 fusion.2
  276.8 1.4 fusion.38
  278.2 2.1 fusion.41
  280.3 2.4 fusion.34
  284.2 31.0 %all_to_all.60 = bf16[16,2,8192]{2,1,0:T(2,128)(2,1)S(1)} all-to-all(bf16[16,2,8192]{2,1,0:T(2,128)(2,1)S(1)} %reshape.326), channel_id=1, replica_groups=mesh['seq'=16,'pipe'=16] {'seq'}, dimensions={0} | all-to-all | bytes 1048576 | tf_op jit(solution)/shard_map/all_to_all | solution.py:114
  317.3 4.7 fusion.17
  322.1 1.6 select_bitcast_fusion
  323.7 21.5 %collective-permute-done = bf16[128,2048]{1,0:T(8,128)(2,1)S(1)} collective-permute-done((bf16[128,2048]{1,0:T(8,128)(2,1)S(1)}, bf16[128,2048]{1,0:T(8,128)(2,1)S(1)}, u32[]{:S(2)}, u32[]{:S(2)}) %collective-permute-start) | collective-permute-done | bytes 524320 | tf_op jit(solution)/shard_map/ppermute | solution.py:16
  345.2 147.4 %all-reduce.2.cloned.1.call-done = bf16[1,128,512]{2,1,0:T(8,128)(2,1)} async-done(((bf16[1,128,512]{2,1,0:T(8,128)(2,1)}), bf16[1,128,512]{2,1,0:T(8,128)(2,1)}) %all-reduce.2.cloned.1.call-update) | async-done | bytes 131088 | tf_op jit(solution)/shard_map/psum | solution.py:11
  493.5 1.6 copy.115
  (76 shorter events, 24.3 us)
Async XLA Ops:
  7.2 75.7 %copy-start.4 = (bf16[1,128,512]{2,1,0:T(8,128)(2,1)S(1)}, bf16[1,128,512]{2,1,0:T(8,128)(2,1)}, u32[]{:S(2)}) copy-start(bf16[1,128,512]{2,1,0:T(8,128)(2,1)} %param.12) | copy-start | bytes 393220
  7.2 70.9 %all-gather.7.cloned.1.call-start = ((), (), s32[]{:S(2)}) async-start(), calls=%async_computation.5 | async-start | bytes 4456448 | tf_op jit(solution)/shard_map/all_gather | solution.py:89
  7.9 182.3 %all-gather.9.cloned.1.call-start = ((), (), s32[]{:S(2)}) async-start(), calls=%async_computation.6 | async-start | bytes 8912896 | tf_op jit(solution)/shard_map/all_gather | solution.py:104
  8.7 308.7 %all-gather.11.cloned.1.call-start = ((), (), s32[]{:S(2)}) async-start(), calls=%async_computation.7 | async-start | bytes 8912896 | tf_op jit(solution)/shard_map/all_gather | solution.py:119
  82.0 0.8 copy-start.1
  83.9 118.7 %all-to-all-start.1 = ((bf16[128,16,64]{0,2,1:T(8,128)(2,1)}), bf16[128,16,64]{0,2,1:T(8,128)(2,1)S(1)}, u32[]{:S(2)}, u32[]{:S(2)}) async-start(bf16[128,16,64]{0,2,1:T(8,128)(2,1)} %bitcast.10), calls=%async_computation.1 | async-start | bytes 524288 | tf_op jit(solution)/shard_map/all_to_all | solution.py:110
  190.2 33.4 %copy-start = (bf16[1,128,2048]{2,1,0:T(8,128)(2,1)S(1)}, bf16[1,128,2048]{2,1,0:T(8,128)(2,1)}, u32[]{:S(2)}) copy-start(bf16[1,128,2048]{2,1,0:T(8,128)(2,1)} %param.7) | copy-start | bytes 1572868
  190.2 33.4 %copy-start.7 = (f32[1,2048]{1,0:T(1,128)S(1)}, f32[1,2048]{1,0:T(1,128)}, u32[]{:S(2)}) copy-start(f32[1,2048]{1,0:T(1,128)} %param.8) | copy-start | bytes 24580
  203.4 29.4 %all-to-all-start = ((bf16[128,16,64]{0,2,1:T(8,128)(2,1)}), bf16[128,16,64]{0,2,1:T(8,128)(2,1)S(1)}, u32[]{:S(2)}, u32[]{:S(2)}) async-start(bf16[128,16,64]{0,2,1:T(8,128)(2,1)} %bitcast.6), calls=%async_computation | async-start | bytes 524288 | tf_op jit(solution)/shard_map/all_to_all | solution.py:111
  232.8 31.5 %all-to-all-start.2 = ((bf16[128,32,64]{0,2,1:T(8,128)(2,1)}), bf16[128,32,64]{0,2,1:T(8,128)(2,1)}, u32[]{:S(2)}, u32[]{:S(2)}) async-start(bf16[128,32,64]{0,2,1:T(8,128)(2,1)} %pad_maximum_fusion), calls=%async_computation.2 | async-start | bytes 1048576 | tf_op jit(solution)/shard_map/all_to_all | solution.py:109
  248.1 244.6 %all-reduce.2.cloned.1.call-start = ((), (), s32[]{:S(2)}) async-start(), calls=%async_computation.4 | async-start | bytes 262144 | tf_op jit(solution)/shard_map/psum | solution.py:11
  264.3 3.1 copy-start.5
  267.1 1.3 copy-start.6
  268.9 1.0 copy-start.3
  276.8 1.4 copy-start.2
  322.0 23.2 %collective-permute-start = (bf16[128,2048]{1,0:T(8,128)(2,1)S(1)}, bf16[128,2048]{1,0:T(8,128)(2,1)S(1)}, u32[]{:S(2)}, u32[]{:S(2)}) collective-permute-start(bf16[128,2048]{1,0:T(8,128)(2,1)S(1)} %fusion.17), channel_id=1, source_target_pairs={{0,1},{1,2},{2,3},{3,4},{4,5},{5,6},{6,7},{7,8},{8,9},{9,10},{10,1... | collective-permute-start | bytes 1572872 | tf_op jit(solution)/shard_map/ppermute | solution.py:16
Sparse Core Ops, SparseCore 0:
  10.7 67.3 all-gather.6
  80.7 109.4 all-gather.8
  192.9 124.3 all-gather.10
  323.9 168.7 all-reduce.1
where the time goes:
time: 505 us; the launch traced here: 502 us
  waiting for transfers between devices  330 us (65%)
  starting transfers between devices  51.2 us (10%)
  local copies, waits for them, and re-layouts  36.6 us (7%)
  blocking collectives  31 us (6%)
  matrix products  26.5 us (5%)
  between operations  14.1 us (3%)
  other arithmetic  11.8 us (2%)
    psum x1, waiting for transfers between devices, from_root(): return lax.psum(jnp.where(mine, x, jnp.zeros_like(x)), axis)  147 us
    all_gather x1, waiting for transfers between devices, per_device(): lax.all_gather(query_weight[0], 'seq', axis=1, tiled=True)  89.7 us
    all_gather x1, waiting for transfers between devices, per_device(): keyval = project(lax.all_gather(kv_weight[0], 'seq', axis=1, tiled=True))  66.5 us
    all_to_all x1, blocking collectives, per_device(): lax.all_to_all(attended, 'seq', split_axis=0, concat_axis=1, tiled=True)  31 us
    ppermute x1, waiting for transfers between devices, passed_along(): return lax.ppermute(x, axis, [(i, (i + by) % peers) for i in range(peers)])  21.5 us
    all_to_all x1, starting transfers between devices, per_device(): lax.all_to_all(values_wide, 'seq', split_axis=1, concat_axis=0, tiled=True)  20.2 us
    all_to_all x1, starting transfers between devices, per_device(): lax.all_to_all(queries, 'seq', split_axis=1, concat_axis=0, tiled=True)  15.3 us
    all_to_all x1, starting transfers between devices, per_device(): lax.all_to_all(keys_wide, 'seq', split_axis=1, concat_axis=0, tiled=True)  15.3 us
  transfers between devices with their start and end apart: 8, of which 6 were waited for; matrix products, arithmetic and copies ran while one was open for 13% of the time, Pallas kernels for 0%

commit v1 on v0

v1 whole, which is shorter than its diff:
```python
import functools

import jax
import jax.numpy as jnp
from jax import lax
from jax.experimental import pallas as pl
from jax.experimental.pallas import tpu as pltpu
from jax.sharding import Mesh
from jax.sharding import PartitionSpec as P

HALVES, RING, CORES, XS, ZS = 2, 4, 2, 4, 4
SEQ = ("zh", "y", "c")
PIPE = ("x", "zl")
rope_base = 500000.0
F32 = jnp.float32
BF16 = jnp.bfloat16
CHUNK = 256


def normalize(inputs, gain):
    wide = inputs.astype(F32)
    scale = lax.rsqrt(jnp.mean(wide * wide, axis=-1, keepdims=True) + 1e-05)
    return (wide * scale * gain).astype(BF16)


def pull(x, axis, by):
    n = lax.axis_size(axis)
    return lax.ppermute(x, axis, [((i + by) % n, i) for i in range(n)])


def rope_tables(positions, head_dim):
    half = head_dim // 2
    freq = rope_base ** (-2.0 * jnp.arange(half, dtype=F32) / head_dim)
    angle = positions.astype(F32)[:, None] * freq
    cosine, sine = jnp.cos(angle), jnp.sin(angle)
    return (
        jnp.concatenate([cosine] * 4, axis=-1),
        jnp.concatenate([-sine, sine, -sine, sine], axis=-1),
    )


def rope(u, cosine, sine):
    lanes = lax.broadcasted_iota(jnp.int32, u.shape, 1)
    swapped = jnp.where(lanes % 64 < 32, pltpu.roll(u, 96, 1), pltpu.roll(u, 32, 1))
    return u * cosine + swapped * sine


def keyval_kernel(place, x, wa, wb, pa, pb, cos, sin, first, mix, kv_out, val_out, w):
    y, h, c, section = place[0], place[1], place[2], place[3]
    w[0:64], w[64:128], w[128:192], w[192:256] = wa[...], pa[...], wb[...], pb[...]
    both = lax.dot_general(x[...], w[...], (((1,), (1,)), ((), ())), preferred_element_type=F32)
    rows = 128
    for slot in range(RING):
        part = both[slot * rows : (slot + 1) * rows]
        own, other = part[:, :128], part[:, 128:]
        keys = jnp.where(h == 0, own, other)
        values = jnp.where(h == 0, other, own)
        keys = jnp.where(c == 0, keys, pltpu.roll(keys, 64, 1))
        values = jnp.where(c == 0, values, pltpu.roll(values, 64, 1))
        rounded = values.astype(BF16)
        wide = rounded.astype(F32)
        before = jnp.where(section == 0, wide, first[slot].astype(F32))
        mixed = mix[0:1, :] * wide + (1.0 - mix[0:1, :]) * before
        keys = rope(keys, cos[slot], sin[slot])
        lanes = lax.broadcasted_iota(jnp.int32, keys.shape, 1)
        low = jnp.where(lanes < 64, keys, pltpu.roll(mixed, 64, 1))
        high = jnp.where(lanes < 64, pltpu.roll(keys, 64, 1), mixed)
        at = lax.rem(y + slot, RING)
        kv_out[at, :, 0:128] = low.astype(BF16)
        kv_out[at, :, 128:256] = high.astype(BF16)
        val_out[slot] = rounded


def query_kernel(x, wa, wb, cos, sin, out, w):
    w[:, :128], w[:, 128:] = wa[...], wb[...]
    both = jnp.dot(x[...], w[...], preferred_element_type=F32)
    for slot in range(RING):
        part = both[slot * 128 : (slot + 1) * 128]
        for pair in range(2):
            u = rope(part[:, pair * 128 : (pair + 1) * 128], cos[slot], sin[slot])
            out[slot, :, pair * 128 : (pair + 1) * 128] = (u * 0.125).astype(BF16)


def attend_kernel(place, q, kv, out, keys, vals, scores, q4):
    step = pl.program_id(0)
    h, c = place[1], place[2]
    lanes = lax.broadcasted_iota(jnp.int32, (128, 128), 1)

    @pl.when(step == 0)
    def _():
        both = kv[...].astype(F32)
        turned = pltpu.roll(both, 64, 1)
        lane = lax.broadcasted_iota(jnp.int32, both.shape, 1)
        keys[...] = jnp.where(lane < 64, both, turned).astype(BF16)
        vals[...] = jnp.where(lane < 64, turned, 1.0).astype(BF16)

    for pair in range(2):
        block = q[0, :, pair * 128 : (pair + 1) * 128].astype(F32)
        q4[pair * 256 : pair * 256 + 128] = jnp.where(lanes < 64, block, 0.0).astype(BF16)
        q4[pair * 256 + 128 : pair * 256 + 256] = jnp.where(lanes < 64, 0.0, block).astype(BF16)
    count = h * 4 + step + 1

    def dots(j):
        chunk = keys[pl.ds(pl.multiple_of(j * CHUNK, CHUNK), CHUNK), :]
        return lax.dot_general(q4[...], chunk, (((1,), (1,)), ((), ())), preferred_element_type=F32)

    s = dots(count - 1)
    row = lax.rem(lax.broadcasted_iota(jnp.int32, s.shape, 0), 128) + c * 128
    col = lax.broadcasted_iota(jnp.int32, s.shape, 1)
    s = jnp.where(col <= row, s, -1e30)
    scores[count - 1] = s
    top = jnp.maximum(s[:, :128], s[:, 128:])

    def first_pass(j, top):
        s = dots(j)
        scores[j] = s
        return jnp.maximum(top, jnp.maximum(s[:, :128], s[:, 128:]))

    top = lax.fori_loop(0, count - 1, first_pass, top)
    top = jnp.max(top, axis=1, keepdims=True)

    def second_pass(j, acc):
        p = jnp.exp(scores[j] - top).astype(BF16)
        chunk = vals[pl.ds(pl.multiple_of(j * CHUNK, CHUNK), CHUNK), :]
        return acc + jnp.dot(p, chunk, preferred_element_type=F32)

    acc = lax.fori_loop(0, count, second_pass, jnp.zeros((512, 128), F32))
    result = acc / pltpu.roll(acc, 64, 1)
    for pair in range(2):
        left = result[pair * 256 : pair * 256 + 128]
        right = pltpu.roll(result[pair * 256 + 128 : pair * 256 + 256], 64, 1)
        out[0, :, pair * 128 : (pair + 1) * 128] = jnp.where(lanes < 64, left, right).astype(BF16)


def out_kernel(base, *refs):
    att, weights, out = refs[:4], refs[4:12], refs[12]
    total = base[...].astype(F32)
    for k in range(4):
        for pair in range(2):
            total += jnp.dot(
                att[k][:, pair * 128 : (pair + 1) * 128], weights[2 * k + pair][...], preferred_element_type=F32
            )
    out[...] = total.astype(out.dtype)


def params(mib):
    return pltpu.CompilerParams(vmem_limit_bytes=mib * 2**20)


VM = pl.BlockSpec(memory_space=pltpu.VMEM)
SM = pl.BlockSpec(memory_space=pltpu.SMEM)


def keyval(place, x, wa, wb, pa, pb, cos, sin, first, mix):
    return pl.pallas_call(
        keyval_kernel,
        out_shape=(jax.ShapeDtypeStruct((4, 128, 256), BF16), jax.ShapeDtypeStruct((4, 128, 128), BF16)),
        in_specs=[SM] + [VM] * 9,
        out_specs=(VM, VM),
        scratch_shapes=[pltpu.VMEM((256, 2048), BF16)],
        compiler_params=params(24),
        cost_estimate=pl.CostEstimate(flops=2 * 512 * 2048 * 256, bytes_accessed=4 << 20, transcendentals=0),
    )(place, x, wa, wb, pa, pb, cos, sin, first, mix)


def query(x, wa, wb, cos, sin):
    return pl.pallas_call(
        query_kernel,
        out_shape=jax.ShapeDtypeStruct((4, 128, 256), BF16),
        in_specs=[VM] * 5,
        out_specs=VM,
        scratch_shapes=[pltpu.VMEM((2048, 256), BF16)],
        compiler_params=params(24),
        cost_estimate=pl.CostEstimate(flops=2 * 512 * 2048 * 256, bytes_accessed=4 << 20, transcendentals=0),
    )(x, wa, wb, cos, sin)


def attend(place, q, kv):
    def at(step, place):
        return (lax.rem(step - place[0] + RING, RING), 0, 0)

    return pl.pallas_call(
        attend_kernel,
        out_shape=jax.ShapeDtypeStruct((4, 128, 256), BF16),
        grid_spec=pltpu.PrefetchScalarGridSpec(
            num_scalar_prefetch=1,
            grid=(RING,),
            in_specs=[
                pl.BlockSpec((1, 128, 256), at),
                pl.BlockSpec((2048, 128), lambda step, place: (0, 0)),
            ],
            out_specs=pl.BlockSpec((1, 128, 256), at),
            scratch_shapes=[
                pltpu.VMEM((2048, 128), BF16),
                pltpu.VMEM((2048, 128), BF16),
                pltpu.VMEM((8, 512, CHUNK), F32),
                pltpu.VMEM((512, 128), BF16),
            ],
        ),
        compiler_params=params(24),
        cost_estimate=pl.CostEstimate(flops=2 * 2 * 512 * 128 * 6656, bytes_accessed=2 << 20, transcendentals=512 * 6656),
    )(place, q, kv)


def project_out(base, att, weights, dtype):
    return pl.pallas_call(
        out_kernel,
        out_shape=jax.ShapeDtypeStruct(base.shape, dtype),
        in_specs=[VM] * 13,
        out_specs=VM,
        compiler_params=params(24),
        cost_estimate=pl.CostEstimate(flops=2 * 128 * 1024 * 2048, bytes_accessed=6 << 20, transcendentals=0),
    )(base, *att, *weights)


def per_device(acts, norm_gain, query_weight, kv_weight, out_weight, first_values, mix_weight):
    inputs = acts[0]
    tok = inputs.shape[0]
    h, y, c = lax.axis_index("zh"), lax.axis_index("y"), lax.axis_index("c")
    section = lax.axis_index("x") * ZS + lax.axis_index("zl")
    place = jnp.stack([y, h, c, section]).astype(jnp.int32)
    core = functools.partial(pull, axis="c", by=1)
    half = functools.partial(pull, axis="zh", by=1)

    w_kv = kv_weight[0].T
    home = [(s, s // 8 * 8 + s % 4 * 2 + s % 8 // 4) for s in range(16)]
    kv_a = lax.ppermute(w_kv, SEQ, home)
    kv_b = lax.ppermute(w_kv, SEQ, [(s, (d + 8) % 16) for s, d in home])
    kv_pa, kv_pb = core(kv_a), core(kv_b)

    normed = normalize(inputs, norm_gain[0])
    x = jnp.concatenate([normed] + [pull(normed, "y", k) for k in range(1, RING)], axis=0)

    w_q = query_weight[0]
    q_c = core(w_q)
    q_z = half(w_q)
    q_zc = core(q_z)

    slots = [lax.rem(y + k, RING) for k in range(RING)]
    positions = jnp.concatenate([(h * 8 + s * 2 + c) * tok + jnp.arange(tok, dtype=jnp.int32) for s in slots])
    cos, sin = (t.reshape(RING, tok, 128) for t in rope_tables(positions, 64))

    cached = jnp.transpose(first_values[0].reshape(tok, 2, RING, 64), (2, 0, 1, 3)).reshape(RING, tok, 128)
    pieces = [lax.dynamic_index_in_dim(cached, y, 0, keepdims=False)]
    for k in range(1, RING):
        pieces.append(pull(lax.dynamic_index_in_dim(cached, lax.rem(y + RING - k, RING), 0, keepdims=False), "y", k))
    first = jnp.stack(pieces)
    mix_two = lax.dynamic_index_in_dim(mix_weight[0].reshape(2, RING), y, 1, keepdims=False)
    mix = jnp.broadcast_to(jnp.repeat(mix_two, 64)[None, :], (8, 128))

    kv, values = keyval(place, x, kv_a, kv_b, kv_pa, kv_pb, cos, sin, first, mix)

    def paired(mine, theirs):
        pair = jnp.where(c == 0, jnp.stack([mine, theirs], 1), jnp.stack([theirs, mine], 1))
        return pair.reshape(RING * 2 * tok, 256)

    kv_before = lax.ppermute(kv, "zh", [(0, 1)])
    own = paired(kv, core(kv))
    before = paired(kv_before, core(kv_before))
    kv_all = jnp.concatenate([jnp.where(h == 0, own, before), own], axis=0)
    kv_low, kv_high = kv_all[:, :128], kv_all[:, 128:]
    kv_near = jnp.where(h == 0, kv_low, kv_high)
    kv_far = jnp.where(h == 0, kv_high, kv_low)

    q_near = query(x, w_q, q_c, cos, sin)
    att_near = attend(place, q_near, kv_near)
    near = [att_near[0]] + [pull(att_near[k], "y", RING - k) for k in range(1, RING)]

    q_far = query(x, q_z, q_zc, cos, sin)
    att_far = attend(place, q_far, kv_far)
    far = [att_far[0]] + [pull(att_far[k], "y", RING - k) for k in range(1, RING)]

    def rows_of(w):
        blocks = [w] + [pull(w, "y", RING - k) for k in range(1, RING)]
        return [b for block in blocks for b in (block, core(block))]

    w_o = out_weight[0]
    total = project_out(inputs, near, rows_of(w_o), F32)
    layer_out = project_out(total, far, rows_of(half(w_o)), BF16)
    passed = pull(layer_out, PIPE, XS * ZS - 1)

    back = [values[0]] + [pull(values[k], "y", RING - k) for k in range(1, RING)]
    turned = jnp.stack(back[::-1])
    turned = jnp.roll(turned, y + 1, axis=0).reshape(RING, tok, 2, 64)
    fresh = jnp.transpose(turned, (1, 2, 0, 3)).reshape(tok, 512)
    fresh = jnp.where(section == 0, fresh, jnp.zeros_like(fresh))
    for pairs in (
        [(0, 2)],
        [(0, 1), (2, 3)],
        [(p, p + 4) for p in range(4)],
        [(p, p + 12) for p in range(4)] + [(p + 4, p + 8) for p in range(4)],
    ):
        fresh = fresh + lax.ppermute(fresh, PIPE, pairs)
    return (passed[None], fresh[None])


def solution(mesh):
    split = Mesh(mesh.devices.reshape(HALVES, RING, CORES, XS, ZS), SEQ + PIPE)
    placed = (
        P(PIPE, SEQ, None),
        P(PIPE, None),
        P(PIPE, None, SEQ),
        P(PIPE, None, SEQ),
        P(PIPE, SEQ, None),
        P(PIPE, SEQ, None),
        P(PIPE, None),
    )
    return jax.shard_map(
        per_device,
        mesh=split,
        in_specs=placed,
        out_specs=(P(PIPE, SEQ, None), P(PIPE, SEQ, None)),
        check_vma=False,
    )
```

time: 505 us -> 215 us (0.43)
  waiting for transfers between devices: 330 us -> 72.2 us
  Pallas kernels: 0 us -> 39.3 us
  blocking collectives: 31 us -> 0 us
  starting transfers between devices: 51.2 us -> 81.4 us
  local copies, waits for them, and re-layouts: 36.6 us -> 7.66 us
  matrix products: 26.5 us -> 0 us
  between operations: 14.1 us -> 1.18 us
    all_gather x3 -> x0, waiting for transfers between devices: 157 us -> none  [the longest x1 89.7 us: per_device(): lax.all_gather(query_weight[0], 'seq', axis=1, tiled=True)]
    psum x1 -> x0, waiting for transfers between devices: 147 us -> none  [from_root(): return lax.psum(jnp.where(mine, x, jnp.zeros_like(x)), axis)]
    ppermute x1 -> x45, starting transfers between devices: 0.08 us -> 81.4 us  [the longest x38 64.7 us: pull(): return lax.ppermute(x, axis, [((i + by) % n, i) for i in range(n)])]
    all_to_all x3 -> x0, starting transfers between devices: 50.8 us -> none  [the longest x1 20.2 us: per_device(): lax.all_to_all(values_wide, 'seq', split_axis=1, concat_axis=0, tiled=True)]
    ppermute x1 -> x45, waiting for transfers between devices: 21.5 us -> 72.2 us  [the longest x38 41.5 us: pull(): return lax.ppermute(x, axis, [((i + by) % n, i) for i in range(n)])]
    pallas_call x0 -> x7, Pallas kernels: none -> 39.3 us  [the longest x2 30.3 us: attend(): pl.pallas_call(attend_kernel, out_shape=jax.ShapeDtypeStruct((4, 128, 256...]
    all_to_all x1 -> x0, blocking collectives: 31 us -> none  [per_device(): lax.all_to_all(attended, 'seq', split_axis=0, concat_axis=1, tiled=True)]
    dot_general x11 -> x0, matrix products: 26.5 us -> none  [the longest x2 9.74 us: project(): return jnp.dot(normed, piece, preferred_element_type=jnp.float32)]
  transfers between devices with their start and end apart: 8 -> 45, of which waited for: 6 -> 13; matrix products, arithmetic and copies ran while one was open for 13% -> 6% of each run, Pallas kernels for 0% -> 19%
where the time goes in v1:
time: 215 us; the launch traced here: 212 us
  starting transfers between devices  81.4 us (38%)
  waiting for transfers between devices  72.2 us (34%)
  Pallas kernels  39.3 us (18%)
  other arithmetic  10.4 us (5%)
  local copies, waits for them, and re-layouts  7.66 us (4%)
    ppermute x38, starting transfers between devices, pull(): return lax.ppermute(x, axis, [((i + by) % n, i) for i in range(n)])  64.7 us
    ppermute x38, waiting for transfers between devices, pull(): return lax.ppermute(x, axis, [((i + by) % n, i) for i in range(n)])  41.5 us
    pallas_call x2, Pallas kernels, attend(): pl.pallas_call(attend_kernel, out_shape=jax.ShapeDtypeStruct((4, 128, 256...  30.3 us
    ppermute x4, waiting for transfers between devices, per_device(): fresh = fresh + lax.ppermute(fresh, PIPE, pairs)  13.2 us
    ppermute x1, waiting for transfers between devices, per_device(): kv_b = lax.ppermute(w_kv, SEQ, [(s, (d + 8) % 16) for s, d in home])  12.7 us
    ppermute x4, starting transfers between devices, per_device(): fresh = fresh + lax.ppermute(fresh, PIPE, pairs)  10.6 us
    unnamed x28, local copies, waits for them, and re-layouts  5.05 us
    ppermute x1, starting transfers between devices, per_device(): kv_a = lax.ppermute(w_kv, SEQ, home)  4.75 us
  transfers between devices with their start and end apart: 45, of which 13 were waited for; matrix products, arithmetic and copies ran while one was open for 6% of the time, Pallas kernels for 19%

profile of v1, /device:TPU:136, one launch (start us, length us, event | category | flops | bytes accessed | tf_op | source)
XLA Modules:
  0.0 212.2 jit_solution(18040544541675142335)
XLA Ops:
  3.7 2.6 %collective-permute-start.1 = (bf16[128,2048]{1,0:T(8,128)(2,1)S(1)}, bf16[128,2048]{1,0:T(8,128)(2,1)S(1)}, u32[]{:S(2)}, u32[]{:S(2)}) collective-permute-start(bf16[128,2048]{1,0:T(8,128)(2,1)S(1)} %fusion.2), channel_id=1, source_target_pairs={{64,0},{96,32},{0,64},{32,96},{65,1},{97,33},{1,65},{33,97},{66,2}... | collective-permute-start | bytes 1572872 | tf_op jit(solution)/shard_map/ppermute | solution.py:28
  6.3 1.9 collective-permute-start.2
  12.3 14.9 %collective-permute-done.8 = bf16[128,128]{1,0:T(8,128)(2,1)S(1)} collective-permute-done((bf16[128,128]{1,0:T(8,128)(2,1)S(1)}, bf16[128,128]{1,0:T(8,128)(2,1)S(1)}, u32[]{:S(2)}, u32[]{:S(2)}) %collective-permute-start.8) | collective-permute-done | bytes 32800 | tf_op jit(solution)/shard_map/ppermute | solution.py:28
  27.3 3.6 %collective-permute-start.10 = (bf16[128,128]{1,0:T(8,128)(2,1)S(1)}, bf16[128,128]{1,0:T(8,128)(2,1)}, u32[]{:S(2)}, u32[]{:S(2)}) collective-permute-start(bf16[128,128]{1,0:T(8,128)(2,1)S(1)} %bitcast.85), channel_id=1, source_target_pairs={{96,0},{0,32},{32,64},{64,96},{97,1},{1,33},{33,65},{65,97},{98,2}... | collective-permute-start | bytes 98312 | tf_op jit(solution)/shard_map/ppermute | solution.py:28
  31.1 4.8 %collective-permute-start.4 = (bf16[64,2048]{1,0:T(8,128)(2,1)}, bf16[64,2048]{1,0:T(8,128)(2,1)S(1)}, u32[]{:S(2)}, u32[]{:S(2)}) collective-permute-start(bf16[64,2048]{1,0:T(8,128)(2,1)} %bitcast.90), channel_id=1, source_target_pairs={{0,0},{16,32},{32,64},{48,96},{64,16},{80,48},{96,80},{112,112},{1... | collective-permute-start | bytes 786440 | tf_op jit(solution)/shard_map/ppermute | solution.py:227
  40.1 4.3 %collective-permute-start.24 = (bf16[2048,128]{1,0:T(8,128)(2,1)S(1)}, bf16[2048,128]{1,0:T(8,128)(2,1)}, u32[]{:S(2)}, u32[]{:S(2)}) collective-permute-start(bf16[2048,128]{1,0:T(8,128)(2,1)S(1)} %bitcast.72), channel_id=1, source_target_pairs={{128,0},{0,128},{129,1},{1,129},{130,2},{2,130},{131,3},{3,131},{1... | collective-permute-start | bytes 1572872 | tf_op jit(solution)/shard_map/ppermute | solution.py:28
  44.3 12.7 %collective-permute-done.5.wb = bf16[64,2048]{1,0:T(8,128)(2,1)} collective-permute-done((bf16[64,2048]{1,0:T(8,128)(2,1)}, bf16[64,2048]{1,0:T(8,128)(2,1)}, u32[]{:S(2)}, u32[]{:S(2)}) %collective-permute-start.5) | collective-permute-done | bytes 262176 | tf_op jit(solution)/shard_map/ppermute | solution.py:228
  59.2 1.7 pad_maximum_fusion.x
  60.8 3.2 %collective-permute-start.20 = (bf16[128,2048]{1,0:T(8,128)(2,1)}, bf16[128,2048]{1,0:T(8,128)(2,1)}, u32[]{:S(2)}, u32[]{:S(2)}) collective-permute-start(bf16[128,2048]{1,0:T(8,128)(2,1)} %bitcast.30.refs_4_), channel_id=1, source_target_pairs={{64,0},{96,32},{0,64},{32,96},{65,1},{97,33},{1,65},{33,97},{66,2}... | collective-permute-start | bytes 1572872 | tf_op jit(solution)/shard_map/ppermute | solution.py:28
  64.1 2.0 shard_map.87
  66.1 1.9 collective-permute-start.38
  69.1 8.8 %collective-permute-done.38 = bf16[128,128]{1,0:T(8,128)(2,1)S(1)} collective-permute-done((bf16[128,128]{1,0:T(8,128)(2,1)S(1)}, bf16[128,128]{1,0:T(8,128)(2,1)S(1)}, u32[]{:S(2)}, u32[]{:S(2)}) %collective-permute-start.38) | collective-permute-done | bytes 32800 | tf_op jit(solution)/shard_map/ppermute | solution.py:28
  79.8 4.5 %collective-permute-done.40 = bf16[128,128]{1,0:T(8,128)(2,1)S(1)} collective-permute-done((bf16[128,128]{1,0:T(8,128)(2,1)S(1)}, bf16[128,128]{1,0:T(8,128)(2,1)S(1)}, u32[]{:S(2)}, u32[]{:S(2)}) %collective-permute-start.40) | collective-permute-done | bytes 32800 | tf_op jit(solution)/shard_map/ppermute | solution.py:28
  84.4 4.2 %collective-permute-start.22 = (bf16[128,2048]{1,0:T(8,128)(2,1)}, bf16[128,2048]{1,0:T(8,128)(2,1)S(1)}, u32[]{:S(2)}, u32[]{:S(2)}) collective-permute-start(bf16[128,2048]{1,0:T(8,128)(2,1)} %bitcast.30.refs_4_), channel_id=1, source_target_pairs={{32,0},{64,32},{96,64},{0,96},{33,1},{65,33},{97,65},{1,97},{34,2}... | collective-permute-start | bytes 1572872 | tf_op jit(solution)/shard_map/ppermute | solution.py:28
  88.6 3.6 %collective-permute-done.12 = bf16[4,128,256]{2,1,0:T(8,128)(2,1)} collective-permute-done((bf16[4,128,256]{2,1,0:T(8,128)(2,1)S(1)}, bf16[4,128,256]{2,1,0:T(8,128)(2,1)}, u32[]{:S(2)}, u32[]{:S(2)}) %collective-permute-start.12) | collective-permute-done | bytes 262176 | tf_op jit(solution)/shard_map/ppermute | solution.py:257
  98.0 3.9 %collective-permute-start.29 = (bf16[128,2048]{1,0:T(8,128)(2,1)}, bf16[128,2048]{1,0:T(8,128)(2,1)S(1)}, u32[]{:S(2)}, u32[]{:S(2)}) collective-permute-start(bf16[128,2048]{1,0:T(8,128)(2,1)} %bitcast.30.refs_4_), channel_id=1, source_target_pairs={{128,0},{0,128},{129,1},{1,129},{130,2},{2,130},{131,3},{3,131},{1... | collective-permute-start | bytes 1572872 | tf_op jit(solution)/shard_map/ppermute | solution.py:28
  102.5 5.6 %collective-permute-start.41 = (bf16[128,512]{0,1:T(8,128)(2,1)S(1)}, bf16[128,512]{0,1:T(8,128)(2,1)S(1)}, u32[]{:S(2)}, u32[]{:S(2)}) collective-permute-start(bf16[128,512]{0,1:T(8,128)(2,1)S(1)} %bitcast.77), channel_id=1, source_target_pairs={{0,2},{16,18},{32,34},{48,50},{64,66},{80,82},{96,98},{112,114},{1... | collective-permute-start | bytes 393224 | tf_op jit(solution)/shard_map/ppermute | solution.py:293
  108.4 2.2 %shard_map.90.q = bf16[4,128,256]{2,1,0:T(8,128)(2,1)S(1)} custom-call(bf16[512,2048]{1,0:T(8,128)(2,1)S(1)} %pad_maximum_fusion.x, bf16[2048,128]{1,0:T(8,128)(2,1)} %collective-permute-done.24.wa, bf16[2048,128]{1,0:T(8,128)(2,1)} %collective-permute-done.25.wb, f32[4,128,128]{2,1,0:T(8,128)S(1)} %pad_maximum_fusion.2.cos, ...), custom_call_target="tpu_custom_call" | custom-call | flops 536870912 | bytes 4194304 | tf_op jit(solution)/shard_map/pallas_call | solution.py:167
  110.6 6.4 %collective-permute-done.29.refs_4_ = bf16[128,2048]{1,0:T(8,128)(2,1)S(1)} collective-permute-done((bf16[128,2048]{1,0:T(8,128)(2,1)}, bf16[128,2048]{1,0:T(8,128)(2,1)S(1)}, u32[]{:S(2)}, u32[]{:S(2)}) %collective-permute-start.29) | collective-permute-done | bytes 524320 | tf_op jit(solution)/shard_map/ppermute | solution.py:28
  117.0 17.9 %collective-permute-start.31 = (bf16[128,2048]{1,0:T(8,128)(2,1)S(1)}, bf16[128,2048]{1,0:T(8,128)(2,1)S(1)}, u32[]{:S(2)}, u32[]{:S(2)}) collective-permute-start(bf16[128,2048]{1,0:T(8,128)(2,1)S(1)} %collective-permute-done.29.refs_4_), channel_id=1, source_target_pairs={{96,0},{0,32},{32,64},{64,96},{97,1},{1,33},{33,65},{65,97},{98,2}... | collective-permute-start | bytes 1572872 | tf_op jit(solution)/shard_map/ppermute | solution.py:28
  135.0 3.7 %collective-permute-start.33 = (bf16[128,2048]{1,0:T(8,128)(2,1)S(1)}, bf16[128,2048]{1,0:T(8,128)(2,1)S(1)}, u32[]{:S(2)}, u32[]{:S(2)}) collective-permute-start(bf16[128,2048]{1,0:T(8,128)(2,1)S(1)} %collective-permute-done.29.refs_4_), channel_id=1, source_target_pairs={{64,0},{96,32},{0,64},{32,96},{65,1},{97,33},{1,65},{33,97},{66,2}... | collective-permute-start | bytes 1572872 | tf_op jit(solution)/shard_map/ppermute | solution.py:28
  139.3 15.1 %shard_map.91 = bf16[4,128,256]{2,1,0:T(8,128)(2,1)S(1)} custom-call(s32[4]{0:T(128)S(1)} %pad_add_fusion.place, bf16[4,128,256]{2,1,0:T(8,128)(2,1)S(1)} %shard_map.90.q, bf16[2048,128]{1,0:T(8,128)(2,1)S(1)} %get-tuple-element.8.kv), custom_call_target="tpu_custom_call" | custom-call | flops 1744830464 | bytes 2097152 | tf_op jit(solution)/shard_map/pallas_call | solution.py:182
  154.5 15.1 %shard_map.88 = bf16[4,128,256]{2,1,0:T(8,128)(2,1)S(1)} custom-call(s32[4]{0:T(128)S(1)} %pad_add_fusion.place, bf16[4,128,256]{2,1,0:T(8,128)(2,1)S(1)} %shard_map.86.q, bf16[2048,128]{1,0:T(8,128)(2,1)S(1)} %get-tuple-element.9.kv), custom_call_target="tpu_custom_call" | custom-call | flops 1744830464 | bytes 2097152 | tf_op jit(solution)/shard_map/pallas_call | solution.py:182
  169.6 2.0 collective-permute-start.26
  174.0 1.9 collective-permute-start.14
  177.4 2.5 %collective-permute-start.15 = (bf16[128,256]{1,0:T(8,128)(2,1)S(1)}, bf16[128,256]{1,0:T(8,128)(2,1)S(1)}, u32[]{:S(2)}, u32[]{:S(2)}) collective-permute-start(bf16[128,256]{1,0:T(8,128)(2,1)S(1)} %get-tuple-element.15), channel_id=1, source_target_pairs={{64,0},{96,32},{0,64},{32,96},{65,1},{97,33},{1,65},{33,97},{66,2}... | collective-permute-start | bytes 196616 | tf_op jit(solution)/shard_map/ppermute | solution.py:28
  180.5 3.5 %collective-permute-start.28 = (bf16[128,256]{1,0:T(8,128)(2,1)S(1)}, bf16[128,256]{1,0:T(8,128)(2,1)S(1)}, u32[]{:S(2)}, u32[]{:S(2)}) collective-permute-start(bf16[128,256]{1,0:T(8,128)(2,1)S(1)} %get-tuple-element.10), channel_id=1, source_target_pairs={{32,0},{64,32},{96,64},{0,96},{33,1},{65,33},{97,65},{1,97},{34,2}... | collective-permute-start | bytes 196616 | tf_op jit(solution)/shard_map/ppermute | solution.py:28
  184.0 4.2 %collective-permute-done.16.refs_3_ = bf16[128,256]{1,0:T(8,128)(2,1)S(1)} collective-permute-done((bf16[128,256]{1,0:T(8,128)(2,1)S(1)}, bf16[128,256]{1,0:T(8,128)(2,1)S(1)}, u32[]{:S(2)}, u32[]{:S(2)}) %collective-permute-start.16) | collective-permute-done | bytes 65568 | tf_op jit(solution)/shard_map/ppermute | solution.py:28
  189.6 2.6 %shard_map.89.base = f32[128,2048]{1,0:T(8,128)S(1)} custom-call(bf16[128,2048]{1,0:T(8,128)(2,1)S(1)} %bitcast.71, bf16[128,256]{1,0:T(8,128)(2,1)S(1)} %get-tuple-element.17.refs_0_, bf16[128,256]{1,0:T(8,128)(2,1)S(1)} %collective-permute-done.14.refs_1_, bf16[128,256]{1,0:T(8,128)(2,1)S(1)} %collective-permute-done.15.refs_2_, ...), custom_call_target="tpu_custom_call" | custom-call | flops 536870912 | bytes 6291456 | tf_op jit(solution)/shard_map/pallas_call | solution.py:206
  193.6 2.4 %collective-permute-start.43 = (bf16[128,512]{0,1:T(8,128)(2,1)S(1)}, bf16[128,512]{0,1:T(8,128)(2,1)S(1)}, u32[]{:S(2)}, u32[]{:S(2)}) collective-permute-start(bf16[128,512]{0,1:T(8,128)(2,1)S(1)} %add.167), channel_id=1, source_target_pairs={{0,4},{1,5},{2,6},{3,7},{16,20},{17,21},{18,22},{19,23},{32,36},{3... | collective-permute-start | bytes 393224 | tf_op jit(solution)/shard_map/ppermute | solution.py:293
  196.0 10.7 %collective-permute-done.43 = bf16[128,512]{0,1:T(8,128)(2,1)S(1)} collective-permute-done((bf16[128,512]{0,1:T(8,128)(2,1)S(1)}, bf16[128,512]{0,1:T(8,128)(2,1)S(1)}, u32[]{:S(2)}, u32[]{:S(2)}) %collective-permute-start.43) | collective-permute-done | bytes 131104 | tf_op jit(solution)/shard_map/ppermute | solution.py:293
  208.1 2.5 %collective-permute-done.44 = bf16[128,512]{0,1:T(8,128)(2,1)S(1)} collective-permute-done((bf16[128,512]{0,1:T(8,128)(2,1)S(1)}, bf16[128,512]{0,1:T(8,128)(2,1)S(1)}, u32[]{:S(2)}, u32[]{:S(2)}) %collective-permute-start.44) | collective-permute-done | bytes 131104 | tf_op jit(solution)/shard_map/ppermute | solution.py:293
  (134 shorter events, 33.9 us)
Async XLA Ops:
  3.2 53.9 %collective-permute-start = (bf16[128,2048]{1,0:T(8,128)(2,1)S(1)}, bf16[128,2048]{1,0:T(8,128)(2,1)}, u32[]{:S(2)}, u32[]{:S(2)}) collective-permute-start(bf16[128,2048]{1,0:T(8,128)(2,1)S(1)} %fusion.2), channel_id=1, source_target_pairs={{32,0},{64,32},{96,64},{0,96},{33,1},{65,33},{97,65},{1,97},{34,2}... | collective-permute-start | bytes 1572872 | tf_op jit(solution)/shard_map/ppermute | solution.py:28
  3.7 53.4 %collective-permute-start.1 = (bf16[128,2048]{1,0:T(8,128)(2,1)S(1)}, bf16[128,2048]{1,0:T(8,128)(2,1)S(1)}, u32[]{:S(2)}, u32[]{:S(2)}) collective-permute-start(bf16[128,2048]{1,0:T(8,128)(2,1)S(1)} %fusion.2), channel_id=1, source_target_pairs={{64,0},{96,32},{0,64},{32,96},{65,1},{97,33},{1,65},{33,97},{66,2}... | collective-permute-start | bytes 1572872 | tf_op jit(solution)/shard_map/ppermute | solution.py:28
  6.3 51.3 %collective-permute-start.2 = (bf16[128,2048]{1,0:T(8,128)(2,1)S(1)}, bf16[128,2048]{1,0:T(8,128)(2,1)S(1)}, u32[]{:S(2)}, u32[]{:S(2)}) collective-permute-start(bf16[128,2048]{1,0:T(8,128)(2,1)S(1)} %fusion.2), channel_id=1, source_target_pairs={{96,0},{0,32},{32,64},{64,96},{97,1},{1,33},{33,65},{65,97},{98,2}... | collective-permute-start | bytes 1572872 | tf_op jit(solution)/shard_map/ppermute | solution.py:28
  9.4 17.8 %collective-permute-start.8 = (bf16[128,128]{1,0:T(8,128)(2,1)S(1)}, bf16[128,128]{1,0:T(8,128)(2,1)S(1)}, u32[]{:S(2)}, u32[]{:S(2)}) collective-permute-start(bf16[128,128]{1,0:T(8,128)(2,1)S(1)} %bitcast.84), channel_id=1, source_target_pairs={{32,0},{64,32},{96,64},{0,96},{33,1},{65,33},{97,65},{1,97},{34,2}... | collective-permute-start | bytes 98312 | tf_op jit(solution)/shard_map/ppermute | solution.py:28
  9.8 21.3 %collective-permute-start.9 = (bf16[128,128]{1,0:T(8,128)(2,1)S(1)}, bf16[128,128]{1,0:T(8,128)(2,1)S(1)}, u32[]{:S(2)}, u32[]{:S(2)}) collective-permute-start(bf16[128,128]{1,0:T(8,128)(2,1)S(1)} %bitcast.83), channel_id=1, source_target_pairs={{64,0},{96,32},{0,64},{32,96},{65,1},{97,33},{1,65},{33,97},{66,2}... | collective-permute-start | bytes 98312 | tf_op jit(solution)/shard_map/ppermute | solution.py:28
  31.1 8.9 %collective-permute-start.4 = (bf16[64,2048]{1,0:T(8,128)(2,1)}, bf16[64,2048]{1,0:T(8,128)(2,1)S(1)}, u32[]{:S(2)}, u32[]{:S(2)}) collective-permute-start(bf16[64,2048]{1,0:T(8,128)(2,1)} %bitcast.90), channel_id=1, source_target_pairs={{0,0},{16,32},{32,64},{48,96},{64,16},{80,48},{96,80},{112,112},{1... | collective-permute-start | bytes 786440 | tf_op jit(solution)/shard_map/ppermute | solution.py:227
  35.9 21.2 %collective-permute-start.5 = (bf16[64,2048]{1,0:T(8,128)(2,1)}, bf16[64,2048]{1,0:T(8,128)(2,1)}, u32[]{:S(2)}, u32[]{:S(2)}) collective-permute-start(bf16[64,2048]{1,0:T(8,128)(2,1)} %bitcast.91), channel_id=1, source_target_pairs={{0,128},{16,160},{32,192},{48,224},{64,144},{80,176},{96,208},{112... | collective-permute-start | bytes 786440 | tf_op jit(solution)/shard_map/ppermute | solution.py:228
  40.1 44.3 %collective-permute-start.24 = (bf16[2048,128]{1,0:T(8,128)(2,1)S(1)}, bf16[2048,128]{1,0:T(8,128)(2,1)}, u32[]{:S(2)}, u32[]{:S(2)}) collective-permute-start(bf16[2048,128]{1,0:T(8,128)(2,1)S(1)} %bitcast.72), channel_id=1, source_target_pairs={{128,0},{0,128},{129,1},{1,129},{130,2},{2,130},{131,3},{3,131},{1... | collective-permute-start | bytes 1572872 | tf_op jit(solution)/shard_map/ppermute | solution.py:28
  57.0 11.0 %collective-permute-start.3 = (bf16[2048,128]{1,0:T(8,128)(2,1)S(1)}, bf16[2048,128]{1,0:T(8,128)(2,1)S(1)}, u32[]{:S(2)}, u32[]{:S(2)}) collective-permute-start(bf16[2048,128]{1,0:T(8,128)(2,1)S(1)} %bitcast.73), channel_id=1, source_target_pairs={{16,0},{0,16},{17,1},{1,17},{18,2},{2,18},{19,3},{3,19},{20,4},{4,... | collective-permute-start | bytes 1572872 | tf_op jit(solution)/shard_map/ppermute | solution.py:28
  57.1 40.8 %collective-permute-start.18 = (bf16[128,2048]{1,0:T(8,128)(2,1)}, bf16[128,2048]{1,0:T(8,128)(2,1)}, u32[]{:S(2)}, u32[]{:S(2)}) collective-permute-start(bf16[128,2048]{1,0:T(8,128)(2,1)} %bitcast.30.refs_4_), channel_id=1, source_target_pairs={{96,0},{0,32},{32,64},{64,96},{97,1},{1,33},{33,65},{65,97},{98,2}... | collective-permute-start | bytes 1572872 | tf_op jit(solution)/shard_map/ppermute | solution.py:28
  60.8 41.0 %collective-permute-start.20 = (bf16[128,2048]{1,0:T(8,128)(2,1)}, bf16[128,2048]{1,0:T(8,128)(2,1)}, u32[]{:S(2)}, u32[]{:S(2)}) collective-permute-start(bf16[128,2048]{1,0:T(8,128)(2,1)} %bitcast.30.refs_4_), channel_id=1, source_target_pairs={{64,0},{96,32},{0,64},{32,96},{65,1},{97,33},{1,65},{33,97},{66,2}... | collective-permute-start | bytes 1572872 | tf_op jit(solution)/shard_map/ppermute | solution.py:28
  66.1 11.8 %collective-permute-start.38 = (bf16[128,128]{1,0:T(8,128)(2,1)S(1)}, bf16[128,128]{1,0:T(8,128)(2,1)S(1)}, u32[]{:S(2)}, u32[]{:S(2)}) collective-permute-start(bf16[128,128]{1,0:T(8,128)(2,1)S(1)} %get-tuple-element.20), channel_id=1, source_target_pairs={{32,0},{64,32},{96,64},{0,96},{33,1},{65,33},{97,65},{1,97},{34,2}... | collective-permute-start | bytes 98312 | tf_op jit(solution)/shard_map/ppermute | solution.py:28
  68.0 10.5 %collective-permute-start.39 = (bf16[128,128]{1,0:T(8,128)(2,1)S(1)}, bf16[128,128]{1,0:T(8,128)(2,1)S(1)}, u32[]{:S(2)}, u32[]{:S(2)}) collective-permute-start(bf16[128,128]{1,0:T(8,128)(2,1)S(1)} %get-tuple-element.19), channel_id=1, source_target_pairs={{64,0},{96,32},{0,64},{32,96},{65,1},{97,33},{1,65},{33,97},{66,2}... | collective-permute-start | bytes 98312 | tf_op jit(solution)/shard_map/ppermute | solution.py:28
  78.5 13.7 %collective-permute-start.12 = (bf16[4,128,256]{2,1,0:T(8,128)(2,1)S(1)}, bf16[4,128,256]{2,1,0:T(8,128)(2,1)}, u32[]{:S(2)}, u32[]{:S(2)}) collective-permute-start(bf16[4,128,256]{2,1,0:T(8,128)(2,1)S(1)} %get-tuple-element.4), channel_id=1, source_target_pairs={{0,128},{1,129},{2,130},{3,131},{4,132},{5,133},{6,134},{7,135},{8... | collective-permute-start | bytes 786440 | tf_op jit(solution)/shard_map/ppermute | solution.py:257
  84.4 17.5 %collective-permute-start.22 = (bf16[128,2048]{1,0:T(8,128)(2,1)}, bf16[128,2048]{1,0:T(8,128)(2,1)S(1)}, u32[]{:S(2)}, u32[]{:S(2)}) collective-permute-start(bf16[128,2048]{1,0:T(8,128)(2,1)} %bitcast.30.refs_4_), channel_id=1, source_target_pairs={{32,0},{64,32},{96,64},{0,96},{33,1},{65,33},{97,65},{1,97},{34,2}... | collective-permute-start | bytes 1572872 | tf_op jit(solution)/shard_map/ppermute | solution.py:28
  92.9 9.6 %collective-permute-start.25 = (bf16[2048,128]{1,0:T(8,128)(2,1)}, bf16[2048,128]{1,0:T(8,128)(2,1)}, u32[]{:S(2)}, u32[]{:S(2)}) collective-permute-start(bf16[2048,128]{1,0:T(8,128)(2,1)} %collective-permute-done.24.wa), channel_id=1, source_target_pairs={{16,0},{0,16},{17,1},{1,17},{18,2},{2,18},{19,3},{3,19},{20,4},{4,... | collective-permute-start | bytes 1572872 | tf_op jit(solution)/shard_map/ppermute | solution.py:28
  96.5 38.5 %collective-permute-start.17 = (bf16[128,2048]{1,0:T(8,128)(2,1)}, bf16[128,2048]{1,0:T(8,128)(2,1)S(1)}, u32[]{:S(2)}, u32[]{:S(2)}) collective-permute-start(bf16[128,2048]{1,0:T(8,128)(2,1)} %bitcast.30.refs_4_), channel_id=1, source_target_pairs={{16,0},{0,16},{17,1},{1,17},{18,2},{2,18},{19,3},{3,19},{20,4},{4,... | collective-permute-start | bytes 1572872 | tf_op jit(solution)/shard_map/ppermute | solution.py:28
  98.0 19.1 %collective-permute-start.29 = (bf16[128,2048]{1,0:T(8,128)(2,1)}, bf16[128,2048]{1,0:T(8,128)(2,1)S(1)}, u32[]{:S(2)}, u32[]{:S(2)}) collective-permute-start(bf16[128,2048]{1,0:T(8,128)(2,1)} %bitcast.30.refs_4_), channel_id=1, source_target_pairs={{128,0},{0,128},{129,1},{1,129},{130,2},{2,130},{131,3},{3,131},{1... | collective-permute-start | bytes 1572872 | tf_op jit(solution)/shard_map/ppermute | solution.py:28
  101.9 36.8 %collective-permute-start.19 = (bf16[128,2048]{1,0:T(8,128)(2,1)}, bf16[128,2048]{1,0:T(8,128)(2,1)S(1)}, u32[]{:S(2)}, u32[]{:S(2)}) collective-permute-start(bf16[128,2048]{1,0:T(8,128)(2,1)} %collective-permute-done.18.refs_6_), channel_id=1, source_target_pairs={{16,0},{0,16},{17,1},{1,17},{18,2},{2,18},{19,3},{3,19},{20,4},{4,... | collective-permute-start | bytes 1572872 | tf_op jit(solution)/shard_map/ppermute | solution.py:28
  101.9 36.9 %collective-permute-start.21 = (bf16[128,2048]{1,0:T(8,128)(2,1)}, bf16[128,2048]{1,0:T(8,128)(2,1)S(1)}, u32[]{:S(2)}, u32[]{:S(2)}) collective-permute-start(bf16[128,2048]{1,0:T(8,128)(2,1)} %collective-permute-done.20.refs_8_), channel_id=1, source_target_pairs={{16,0},{0,16},{17,1},{1,17},{18,2},{2,18},{19,3},{3,19},{20,4},{4,... | collective-permute-start | bytes 1572872 | tf_op jit(solution)/shard_map/ppermute | solution.py:28
  102.5 36.2 %collective-permute-start.41 = (bf16[128,512]{0,1:T(8,128)(2,1)S(1)}, bf16[128,512]{0,1:T(8,128)(2,1)S(1)}, u32[]{:S(2)}, u32[]{:S(2)}) collective-permute-start(bf16[128,512]{0,1:T(8,128)(2,1)S(1)} %bitcast.77), channel_id=1, source_target_pairs={{0,2},{16,18},{32,34},{48,50},{64,66},{80,82},{96,98},{112,114},{1... | collective-permute-start | bytes 393224 | tf_op jit(solution)/shard_map/ppermute | solution.py:293
  117.0 54.6 %collective-permute-start.31 = (bf16[128,2048]{1,0:T(8,128)(2,1)S(1)}, bf16[128,2048]{1,0:T(8,128)(2,1)S(1)}, u32[]{:S(2)}, u32[]{:S(2)}) collective-permute-start(bf16[128,2048]{1,0:T(8,128)(2,1)S(1)} %collective-permute-done.29.refs_4_), channel_id=1, source_target_pairs={{96,0},{0,32},{32,64},{64,96},{97,1},{1,33},{33,65},{65,97},{98,2}... | collective-permute-start | bytes 1572872 | tf_op jit(solution)/shard_map/ppermute | solution.py:28
  135.0 38.0 %collective-permute-start.33 = (bf16[128,2048]{1,0:T(8,128)(2,1)S(1)}, bf16[128,2048]{1,0:T(8,128)(2,1)S(1)}, u32[]{:S(2)}, u32[]{:S(2)}) collective-permute-start(bf16[128,2048]{1,0:T(8,128)(2,1)S(1)} %collective-permute-done.29.refs_4_), channel_id=1, source_target_pairs={{64,0},{96,32},{0,64},{32,96},{65,1},{97,33},{1,65},{33,97},{66,2}... | collective-permute-start | bytes 1572872 | tf_op jit(solution)/shard_map/ppermute | solution.py:28
  138.7 34.2 %collective-permute-start.35 = (bf16[128,2048]{1,0:T(8,128)(2,1)S(1)}, bf16[128,2048]{1,0:T(8,128)(2,1)S(1)}, u32[]{:S(2)}, u32[]{:S(2)}) collective-permute-start(bf16[128,2048]{1,0:T(8,128)(2,1)S(1)} %collective-permute-done.29.refs_4_), channel_id=1, source_target_pairs={{32,0},{64,32},{96,64},{0,96},{33,1},{65,33},{97,65},{1,97},{34,2}... | collective-permute-start | bytes 1572872 | tf_op jit(solution)/shard_map/ppermute | solution.py:28
  138.7 34.7 %collective-permute-start.30 = (bf16[128,2048]{1,0:T(8,128)(2,1)S(1)}, bf16[128,2048]{1,0:T(8,128)(2,1)S(1)}, u32[]{:S(2)}, u32[]{:S(2)}) collective-permute-start(bf16[128,2048]{1,0:T(8,128)(2,1)S(1)} %collective-permute-done.29.refs_4_), channel_id=1, source_target_pairs={{16,0},{0,16},{17,1},{1,17},{18,2},{2,18},{19,3},{3,19},{20,4},{4,... | collective-permute-start | bytes 1572872 | tf_op jit(solution)/shard_map/ppermute | solution.py:28
  138.8 30.8 %collective-permute-start.23 = (bf16[128,2048]{1,0:T(8,128)(2,1)S(1)}, bf16[128,2048]{1,0:T(8,128)(2,1)S(1)}, u32[]{:S(2)}, u32[]{:S(2)}) collective-permute-start(bf16[128,2048]{1,0:T(8,128)(2,1)S(1)} %collective-permute-done.22.refs_10_), channel_id=1, source_target_pairs={{16,0},{0,16},{17,1},{1,17},{18,2},{2,18},{19,3},{3,19},{20,4},{4,... | collective-permute-start | bytes 1572872 | tf_op jit(solution)/shard_map/ppermute | solution.py:28
  172.9 19.2 %collective-permute-start.32 = (bf16[128,2048]{1,0:T(8,128)(2,1)S(1)}, bf16[128,2048]{1,0:T(8,128)(2,1)S(1)}, u32[]{:S(2)}, u32[]{:S(2)}) collective-permute-start(bf16[128,2048]{1,0:T(8,128)(2,1)S(1)} %collective-permute-done.31.refs_6_), channel_id=1, source_target_pairs={{16,0},{0,16},{17,1},{1,17},{18,2},{2,18},{19,3},{3,19},{20,4},{4,... | collective-permute-start | bytes 1572872 | tf_op jit(solution)/shard_map/ppermute | solution.py:28
  172.9 19.2 %collective-permute-start.34 = (bf16[128,2048]{1,0:T(8,128)(2,1)S(1)}, bf16[128,2048]{1,0:T(8,128)(2,1)S(1)}, u32[]{:S(2)}, u32[]{:S(2)}) collective-permute-start(bf16[128,2048]{1,0:T(8,128)(2,1)S(1)} %collective-permute-done.33.refs_8_), channel_id=1, source_target_pairs={{16,0},{0,16},{17,1},{1,17},{18,2},{2,18},{19,3},{3,19},{20,4},{4,... | collective-permute-start | bytes 1572872 | tf_op jit(solution)/shard_map/ppermute | solution.py:28
  173.4 18.7 %collective-permute-start.36 = (bf16[128,2048]{1,0:T(8,128)(2,1)S(1)}, bf16[128,2048]{1,0:T(8,128)(2,1)S(1)}, u32[]{:S(2)}, u32[]{:S(2)}) collective-permute-start(bf16[128,2048]{1,0:T(8,128)(2,1)S(1)} %collective-permute-done.35.refs_10_), channel_id=1, source_target_pairs={{16,0},{0,16},{17,1},{1,17},{18,2},{2,18},{19,3},{3,19},{20,4},{4,... | collective-permute-start | bytes 1572872 | tf_op jit(solution)/shard_map/ppermute | solution.py:28
  180.5 11.7 %collective-permute-start.28 = (bf16[128,256]{1,0:T(8,128)(2,1)S(1)}, bf16[128,256]{1,0:T(8,128)(2,1)S(1)}, u32[]{:S(2)}, u32[]{:S(2)}) collective-permute-start(bf16[128,256]{1,0:T(8,128)(2,1)S(1)} %get-tuple-element.10), channel_id=1, source_target_pairs={{32,0},{64,32},{96,64},{0,96},{33,1},{65,33},{97,65},{1,97},{34,2}... | collective-permute-start | bytes 196616 | tf_op jit(solution)/shard_map/ppermute | solution.py:28
  193.4 17.9 %collective-permute-start.37 = (bf16[128,2048]{1,0:T(8,128)(2,1)S(1)}, bf16[128,2048]{1,0:T(8,128)(2,1)S(1)}, u32[]{:S(2)}, u32[]{:S(2)}) collective-permute-start(bf16[128,2048]{1,0:T(8,128)(2,1)S(1)} %shard_map.92), channel_id=1, source_target_pairs={{15,0},{0,1},{1,2},{2,3},{3,4},{4,5},{5,6},{6,7},{7,8},{8,9},{9,10... | collective-permute-start | bytes 1572872 | tf_op jit(solution)/shard_map/ppermute | solution.py:28
  193.6 13.1 %collective-permute-start.43 = (bf16[128,512]{0,1:T(8,128)(2,1)S(1)}, bf16[128,512]{0,1:T(8,128)(2,1)S(1)}, u32[]{:S(2)}, u32[]{:S(2)}) collective-permute-start(bf16[128,512]{0,1:T(8,128)(2,1)S(1)} %add.167), channel_id=1, source_target_pairs={{0,4},{1,5},{2,6},{3,7},{16,20},{17,21},{18,22},{19,23},{32,36},{3... | collective-permute-start | bytes 393224 | tf_op jit(solution)/shard_map/ppermute | solution.py:293
  (21 other events, 257.1 us)
